TPU v7x, 128 devices: a whole 4x4x4 slice. The times are simulated.
128 devices in a mesh: dp: 16 (over x_lo, y, core), tensor: 8 (over x_hi, z).
Axes of the slice: x: 4 (x_hi: 2, x_lo: 2; x = x_hi * 2 + x_lo), y: 4, z: 4, core: 2. Of those that a mesh axis runs over, the one named last changes fastest.
Arguments:
- hidden: bfloat16 [12288, 12288], P('dp', 'tensor'), may hold values from -6 to 6
- residual_in: bfloat16 [12288, 6144], P('dp', 'tensor'), may hold values from -6 to 6
- w_down: bfloat16 [12288, 6144], P('tensor', 'dp'), may hold values from -0.0546875 to 0.0546875
- w_key: bfloat16 [6144, 2048], P('tensor', 'dp'), may hold values from -0.078125 to 0.078125
- w_value: bfloat16 [6144, 2048], P('tensor', 'dp'), may hold values from -0.078125 to 0.078125
- queries: float32 [512, 2048], P('dp'), may hold values from -6 to 6
- w_query: bfloat16 [2048, 2048], P(None, 'tensor'), may hold values from -0.125 to 0.125
- attn_bias: float32 [16, 32, 768], P('dp'), as said below
- w_out: bfloat16 [2048, 2048], replicated, may hold values from -0.125 to 0.125
- w_in: bfloat16 [2048, 8192], P(None, 'tensor'), may hold values from -0.125 to 0.125
- w_back: bfloat16 [8192, 2048], P('tensor'), may hold values from -0.0625 to 0.0625
Outputs:
- query_out: bfloat16 [512, 2048], P('dp')
Inputs may be any that keep to these rules, and one draw needn't show every extreme that they name: `attn_bias`: the same bias for every head of an image.
All inputs are finite; a program needn't handle non-finite values.
Results may differ from a plain program's by a relative error of at most 0.024.
Values may be sent and summed in bfloat16 or wider, within the bound.
No kernel may reach another device: no remote copies, remote signals or barrier semaphores. Data moves between devices by JAX's collectives and lax.ppermute only.
A program may use at most 192 MiB of HBM per device.

v0:
```python
import jax
import jax.numpy as jnp
from jax import lax
from jax.sharding import PartitionSpec as P

HEAD_DIM = 128


def layer_norm(x):
    mean = jnp.mean(x, axis=-1, keepdims=True)
    centered = x - mean
    var = jnp.mean(centered * centered, axis=-1, keepdims=True)
    return centered * lax.rsqrt(var + 1e-06)


def shards(
    hidden, residual_in, w_down, w_key, w_value, queries, w_query, attn_bias, w_out, w_in, w_back
):
    tok_rows = hidden.shape[0]
    partial_value = jnp.dot(
        hidden, lax.all_gather(w_down, "dp", axis=1, tiled=True), preferred_element_type=jnp.float32
    )
    summed = lax.psum_scatter(
        partial_value.astype(jnp.bfloat16), "tensor", scatter_dimension=1, tiled=True
    ).astype(jnp.float32)
    features = (residual_in.astype(jnp.float32) + summed).astype(jnp.bfloat16)
    key_part = jnp.dot(
        features,
        lax.all_gather(w_key, "dp", axis=1, tiled=True),
        preferred_element_type=jnp.float32,
    )
    value_part = jnp.dot(
        features,
        lax.all_gather(w_value, "dp", axis=1, tiled=True),
        preferred_element_type=jnp.float32,
    )
    key_part, value_part = (key_part, value_part)
    key_sum, value_sum = (
        lax.psum_scatter(
            key_part.astype(jnp.bfloat16), "tensor", scatter_dimension=1, tiled=True
        ).astype(jnp.float32),
        lax.psum_scatter(
            value_part.astype(jnp.bfloat16), "tensor", scatter_dimension=1, tiled=True
        ).astype(jnp.float32),
    )
    keys = key_sum.astype(jnp.bfloat16)
    vals = value_sum.astype(jnp.bfloat16)
    local_heads = keys.shape[1] // HEAD_DIM
    scale = 1.0 / HEAD_DIM**0.5
    qnorm = layer_norm(queries).astype(jnp.bfloat16)
    qproj = (jnp.dot(qnorm, w_query, preferred_element_type=jnp.float32) * scale).astype(
        jnp.bfloat16
    )
    num_queries = queries.shape[0]
    scores = jnp.einsum(
        "qhd,khd->hqk",
        qproj.reshape(num_queries, local_heads, HEAD_DIM),
        keys.reshape(tok_rows, local_heads, HEAD_DIM),
        preferred_element_type=jnp.float32,
    )
    scores = scores + attn_bias[0][None]
    probs = jax.nn.softmax(scores, axis=-1).astype(jnp.bfloat16)
    attended = jnp.einsum(
        "hqk,khd->qhd",
        probs,
        vals.reshape(tok_rows, local_heads, HEAD_DIM),
        preferred_element_type=jnp.float32,
    ).astype(jnp.bfloat16)
    attended = attended.reshape(num_queries, local_heads * HEAD_DIM)
    whole = lax.all_gather(attended, "tensor", axis=1, tiled=True)
    projected = jnp.dot(whole, w_out, preferred_element_type=jnp.float32)
    mid = queries + projected
    mnorm = layer_norm(mid).astype(jnp.bfloat16)
    inner = jax.nn.gelu(jnp.dot(mnorm, w_in, preferred_element_type=jnp.float32)).astype(
        jnp.bfloat16
    )
    back = lax.psum(
        jnp.dot(inner, w_back, preferred_element_type=jnp.float32).astype(jnp.bfloat16), "tensor"
    ).astype(jnp.float32)
    return (mid + back).astype(jnp.bfloat16)


def solution(mesh):
    in_specs = (
        P("dp", "tensor"),
        P("dp", "tensor"),
        P("tensor", "dp"),
        P("tensor", "dp"),
        P("tensor", "dp"),
        P("dp", None),
        P(None, "tensor"),
        P("dp", None, None),
        P(),
        P(None, "tensor"),
        P("tensor", None),
    )
    out_specs = P("dp", None)
    return jax.shard_map(shards, mesh=mesh, in_specs=in_specs, out_specs=out_specs, check_vma=False)
```

profile of v0, /device:TPU:0, one launch (start us, length us, event | category | flops | bytes accessed | tf_op | source)
XLA Modules:
  0.0 629.7 jit_solution(13739481954018807919)
XLA Ops:
  6.5 0.0 copy-start
  6.5 0.0 all-gather.4.cloned.1.call-start
  6.5 0.7 all-gather.4.cloned.1.call-update
  7.3 0.0 all-gather.8.cloned.1.call-start
  7.3 0.7 all-gather.8.cloned.1.call-update
  8.0 0.0 reduce-scatter.4.cloned.1.call-start
  8.1 104.8 %all-gather.4.cloned.1.call-done = bf16[1536,6144]{1,0:T(8,128)(2,1)} async-done(((bf16[1536,384]{1,0:T(8,128)(2,1)}), bf16[1536,6144]{1,0:T(8,128)(2,1)}) %all-gather.4.cloned.1.call-update) | async-done | bytes 18874384 | tf_op jit(solution)/shard_map/all_gather | solution.py:21
  112.9 0.0 copy-done
  112.9 19.6 %convolution_convert_fusion = bf16[768,6144]{1,0:T(8,128)(2,1)} fusion(bf16[768,1536]{1,0:T(8,128)(2,1)S(1)} %copy-done, bf16[1536,6144]{1,0:T(8,128)(2,1)} %all-gather.4.cloned.1.call-done), kind=kOutput, calls=%fused_computation.1 | convolution fusion | flops 14500233216 | bytes 30670848 | tf_op jit(solution)/shard_map/dot_general | solution.py:20
  132.5 0.0 copy-start.5
  132.5 0.0 reduce-scatter.4.cloned.1.call-update
  132.5 0.0 all-gather.6.cloned.1.call-start
  132.6 0.5 all-gather.6.cloned.1.call-update
  133.1 0.0 reduce-scatter.8.cloned.1.call-start
  133.1 23.5 %all-gather.8.cloned.1.call-done = bf16[768,2048]{1,0:T(8,128)(2,1)} async-done(((bf16[768,128]{1,0:T(8,128)(2,1)}), bf16[768,2048]{1,0:T(8,128)(2,1)}) %all-gather.8.cloned.1.call-update) | async-done | bytes 3145744 | tf_op jit(solution)/shard_map/all_gather | solution.py:29
  156.7 128.9 %reduce-scatter.4.cloned.1.call-done = bf16[768,768]{1,0:T(8,128)(2,1)} async-done(((bf16[768,6144]{1,0:T(8,128)(2,1)}), bf16[768,768]{1,0:T(8,128)(2,1)}) %reduce-scatter.4.cloned.1.call-update) | async-done | bytes 1179664 | tf_op jit(solution)/shard_map/reduce_scatter | solution.py:23
  285.6 0.0 copy-done.5
  285.6 6.6 %convolution_convert_fusion.1 = bf16[768,2048]{1,0:T(8,128)(2,1)} fusion(bf16[768,2048]{1,0:T(8,128)(2,1)} %all-gather.8.cloned.1.call-done, bf16[768,768]{1,0:T(8,128)(2,1)} %reduce-scatter.4.cloned.1.call-done, bf16[768,768]{1,0:T(8,128)(2,1)S(1)} %copy-done.5), kind=kOutput, calls=%fused_computation.2 | convolution fusion | flops 2419851264 | bytes 8650752 | tf_op jit(solution)/shard_map/dot_general | solution.py:27
  292.2 0.0 copy-start.6
  292.2 0.0 reduce-scatter.8.cloned.1.call-update
  292.2 0.0 reduce-scatter.6.cloned.1.call-start
  292.2 33.9 %all-gather.6.cloned.1.call-done = bf16[768,2048]{1,0:T(8,128)(2,1)} async-done(((bf16[768,128]{1,0:T(8,128)(2,1)}), bf16[768,2048]{1,0:T(8,128)(2,1)}) %all-gather.6.cloned.1.call-update) | async-done | bytes 3145744 | tf_op jit(solution)/shard_map/all_gather | solution.py:34
  326.2 0.0 copy-done.6
  326.2 5.9 convolution_convert_fusion.2
  332.1 0.0 copy-start.2
  332.1 0.0 copy-start.3
  332.1 0.0 copy-start.4
  332.1 0.0 reduce-scatter.6.cloned.1.call-update
  332.1 0.0 all-reduce.2.cloned.1.call-start
  332.2 0.9 copy-done.2
  333.0 0.1 reduce_sum.45
  333.2 0.2 multiply_reduce_fusion.1
  333.4 0.0 copy-done.3
  333.4 0.3 fusion.4
  333.7 75.8 %reduce-scatter.8.cloned.1.call-done = bf16[768,256]{1,0:T(8,128)(2,1)} async-done(((bf16[768,2048]{1,0:T(8,128)(2,1)}), bf16[768,256]{1,0:T(8,128)(2,1)}) %reduce-scatter.8.cloned.1.call-update) | async-done | bytes 393232 | tf_op jit(solution)/shard_map/reduce_scatter | solution.py:39
  409.6 0.0 copy-done.4
  409.6 1.2 convolution_add_fusion.1
  410.8 0.2 fusion.37
  411.0 80.6 %reduce-scatter.6.cloned.1.call-done = bf16[768,256]{1,0:T(8,128)(2,1)} async-done(((bf16[768,2048]{1,0:T(8,128)(2,1)}), bf16[768,256]{1,0:T(8,128)(2,1)}) %reduce-scatter.6.cloned.1.call-update) | async-done | bytes 393232 | tf_op jit(solution)/shard_map/reduce_scatter | solution.py:42
  491.6 1.3 fusion.5
  492.8 34.2 %all_gather.15 = bf16[32,2048]{1,0:T(8,128)(2,1)S(1)} all-gather(bf16[32,256]{1,0:T(8,128)(2,1)S(1)} %bitcast.38), channel_id=1, replica_groups=mesh['dp'=16,'tensor'=8] {'tensor'}, dimensions={1}, use_global_device_ids=true | all-gather | bytes 147456 | tf_op jit(solution)/shard_map/all_gather | solution.py:70
  527.0 5.0 fusion.38
  532.1 0.2 multiply_reduce_fusion
  532.3 5.9 convolution_convert_fusion.3
  538.2 0.0 all-reduce.2.cloned.1.call-update
  538.2 83.0 %all-reduce.2.cloned.1.call-done = bf16[32,2048]{1,0:T(8,128)(2,1)} async-done(((bf16[32,2048]{1,0:T(8,128)(2,1)}), bf16[32,2048]{1,0:T(8,128)(2,1)}) %all-reduce.2.cloned.1.call-update) | async-done | bytes 131088 | tf_op jit(solution)/shard_map/psum | solution.py:77
  621.2 1.6 add_convert_fusion.3
  622.8 0.0 copy-done.1
  (6 shorter events, 0.0 us)
Async XLA Ops:
  6.5 106.3 %copy-start = (bf16[768,1536]{1,0:T(8,128)(2,1)S(1)}, bf16[768,1536]{1,0:T(8,128)(2,1)}, u32[]{:S(2)}) copy-start(bf16[768,1536]{1,0:T(8,128)(2,1)} %param.11) | copy-start | bytes 7077892
  6.5 106.3 %all-gather.4.cloned.1.call-start = ((), (), s32[]{:S(2)}) async-start(), calls=%async_computation.3 | async-start | bytes 20054016 | tf_op jit(solution)/shard_map/all_gather | solution.py:21
  7.3 149.4 %all-gather.8.cloned.1.call-start = ((), (), s32[]{:S(2)}) async-start(), calls=%async_computation.7 | async-start | bytes 3342336 | tf_op jit(solution)/shard_map/all_gather | solution.py:29
  8.0 277.6 %reduce-scatter.4.cloned.1.call-start = ((), (), s32[]{:S(2)}) async-start(), calls=%async_computation.4 | async-start | bytes 10616832 | tf_op jit(solution)/shard_map/reduce_scatter | solution.py:23
  132.5 153.1 %copy-start.5 = (bf16[768,768]{1,0:T(8,128)(2,1)S(1)}, bf16[768,768]{1,0:T(8,128)(2,1)}, u32[]{:S(2)}) copy-start(bf16[768,768]{1,0:T(8,128)(2,1)} %param.12) | copy-start | bytes 3538948
  132.5 193.7 %all-gather.6.cloned.1.call-start = ((), (), s32[]{:S(2)}) async-start(), calls=%async_computation.5 | async-start | bytes 3342336 | tf_op jit(solution)/shard_map/all_gather | solution.py:34
  133.1 276.5 %reduce-scatter.8.cloned.1.call-start = ((), (), s32[]{:S(2)}) async-start(), calls=%async_computation.8 | async-start | bytes 3538944 | tf_op jit(solution)/shard_map/reduce_scatter | solution.py:39
  292.2 34.0 %copy-start.6 = (bf16[768,768]{1,0:T(8,128)(2,1)S(1)}, bf16[768,768]{1,0:T(8,128)(2,1)}, u32[]{:S(2)}) copy-start(bf16[768,768]{1,0:T(8,128)(2,1)} %reduce-scatter.4.cloned.1.call-done) | copy-start | bytes 3538948
  292.2 199.4 %reduce-scatter.6.cloned.1.call-start = ((), (), s32[]{:S(2)}) async-start(), calls=%async_computation.6 | async-start | bytes 3538944 | tf_op jit(solution)/shard_map/reduce_scatter | solution.py:42
  332.1 0.9 copy-start.2
  332.1 1.3 copy-start.3
  332.1 77.5 %copy-start.4 = (f32[1,32,768]{2,1,0:T(8,128)S(1)}, f32[1,32,768]{2,1,0:T(8,128)}, u32[]{:S(2)}) copy-start(f32[1,32,768]{2,1,0:T(8,128)} %param.18) | copy-start | bytes 294916
  332.1 289.1 %all-reduce.2.cloned.1.call-start = ((), (), s32[]{:S(2)}) async-start(), calls=%async_computation.9 | async-start | bytes 262144 | tf_op jit(solution)/shard_map/psum | solution.py:77
  532.3 90.5 %copy-start.1 = (bf16[768,1536]{1,0:T(8,128)(2,1)S(1)}, bf16[768,1536]{1,0:T(8,128)(2,1)}, u32[]{:S(2)}) copy-start(bf16[768,1536]{1,0:T(8,128)(2,1)} %param.11) | copy-start | bytes 7077892
Sparse Core Ops, SparseCore 0:
  9.0 103.7 all-gather.3
  114.5 42.1 all-gather.7
  160.5 125.0 reduce-scatter.3
  287.1 39.0 all-gather.5
  329.9 79.6 reduce-scatter.7
  413.3 78.2 reduce-scatter.5
  538.3 82.8 all-reduce.1
where the time goes:
time: 630 us
  waiting for transfers between devices  533 us (85%)
  matrix products  45.8 us (7%)
  blocking collectives  34.2 us (5%)
  between operations  13.5 us (2%)
    reduce_scatter x1, waiting for transfers between devices, shards(): lax.psum_scatter(partial_value.astype(jnp.bfloat16), 'tensor', scatter_di...  129 us
    all_gather x1, waiting for transfers between devices, shards(): lax.all_gather(w_down, 'dp', axis=1, tiled=True)  105 us
    psum x1, waiting for transfers between devices, shards(): lax.psum(jnp.dot(inner, w_back, preferred_element_type=jnp.float32).astyp...  83 us
    reduce_scatter x1, waiting for transfers between devices, shards(): lax.psum_scatter(value_part.astype(jnp.bfloat16), 'tensor', scatter_dimen...  80.6 us
    reduce_scatter x1, waiting for transfers between devices, shards(): lax.psum_scatter(key_part.astype(jnp.bfloat16), 'tensor', scatter_dimensi...  75.8 us
    all_gather x1, blocking collectives, shards(): whole = lax.all_gather(attended, 'tensor', axis=1, tiled=True)  34.2 us
    all_gather x1, waiting for transfers between devices, shards(): lax.all_gather(w_value, 'dp', axis=1, tiled=True)  33.9 us
    all_gather x1, waiting for transfers between devices, shards(): lax.all_gather(w_key, 'dp', axis=1, tiled=True)  23.5 us
  transfers between devices with their start and end apart: 7, of which 7 were waited for; matrix products, arithmetic and copies ran while one was open for 5% of the time, Pallas kernels for 0%

commit v1 on v0

v1 whole, which is shorter than its diff:
```python
import jax
import jax.numpy as jnp
from jax import lax
from jax.sharding import PartitionSpec as P

HEAD_DIM = 128
AXES = ("dp", "tensor")
BF16 = jnp.bfloat16
F32 = jnp.float32


def layer_norm(x):
    mean = jnp.mean(x, axis=-1, keepdims=True)
    centered = x - mean
    var = jnp.mean(centered * centered, axis=-1, keepdims=True)
    return centered * lax.rsqrt(var + 1e-06)


def matmul(a, b):
    return jnp.dot(a, b, preferred_element_type=F32)


def matmul_t(a, b):
    return lax.dot_general(a, b, (((1,), (1,)), ((), ())), preferred_element_type=F32)


def tensor_blocks(x):
    pairs = [[(s, s ^ j) for s in range(8)] for j in range(8)]
    return [x] + [lax.ppermute(x, "tensor", pairs[j]) for j in range(1, 8)]


def tree_sum(blocks):
    while len(blocks) > 1:
        blocks = [a + b for a, b in zip(blocks[::2], blocks[1::2])]
    return blocks[0]


def in_order(blocks):
    me = lax.axis_index("tensor")
    stacked = jnp.stack(blocks)
    return jnp.stack(
        [lax.dynamic_index_in_dim(stacked, me ^ g, 0, keepdims=False) for g in range(8)]
    )


def shards(
    hidden, residual_in, w_down, w_key, w_value, queries, w_query, attn_bias, w_out, w_in, w_back
):
    nq = queries.shape[0]
    ff = hidden.shape[1]
    scale = 1.0 / HEAD_DIM**0.5
    qnorm = layer_norm(queries).astype(BF16)
    qproj = (matmul(qnorm, w_query) * scale).astype(BF16)
    q_heads = in_order(tensor_blocks(qproj))
    q_heads = q_heads.reshape(8, nq, 2, HEAD_DIM).transpose(0, 2, 1, 3).reshape(16 * nq, HEAD_DIM)
    q_all = lax.all_to_all(q_heads, "dp", 0, 0, tiled=True)
    w_kv = jnp.concatenate([w_key, w_value], axis=1)
    down_all = lax.all_gather(w_down, "dp", axis=1, tiled=True)
    kv_all = lax.all_gather(w_kv, "tensor", axis=0, tiled=True)
    w_head = jnp.concatenate([matmul(down_all, kv_all).astype(BF16), w_kv], axis=0)
    q_wide = matmul_t(q_all, w_head[:, :HEAD_DIM]).astype(BF16)
    q_wide = lax.all_to_all(q_wide, "dp", 0, 0, tiled=True)
    part = matmul_t(q_wide[:, :ff], hidden) + matmul_t(q_wide[:, ff:], residual_in)
    part = lax.all_to_all(part.astype(BF16), "tensor", 0, 0, tiled=True)
    scores = jnp.sum(part.reshape(8, 2, nq, -1).astype(F32), axis=0) + attn_bias[0][None]
    probs = jax.nn.softmax(scores, axis=-1).astype(BF16).reshape(2 * nq, -1)
    probs = in_order(tensor_blocks(probs)).reshape(16 * nq, -1)
    wide = jnp.concatenate([matmul(probs, hidden), matmul(probs, residual_in)], axis=1)
    wide = lax.all_to_all(wide.astype(BF16), "dp", 0, 0, tiled=True)
    part = matmul(wide, w_head[:, HEAD_DIM:]).astype(BF16)
    part = lax.all_to_all(part, "dp", 0, 0, tiled=True)
    part = part.reshape(16, nq, HEAD_DIM).transpose(1, 0, 2).reshape(nq, 16 * HEAD_DIM)
    attended = tree_sum([b.astype(F32) for b in tensor_blocks(part)]).astype(BF16)
    mid = queries + matmul(attended, w_out)
    mnorm = layer_norm(mid).astype(BF16)
    inner = jax.nn.gelu(matmul(mnorm, w_in)).astype(BF16)
    back = tensor_blocks(matmul(inner, w_back).astype(BF16))
    return (mid + tree_sum([b.astype(F32) for b in back])).astype(BF16)


def solution(mesh):
    in_specs = (
        P("dp", "tensor"),
        P("dp", "tensor"),
        P("tensor", "dp"),
        P("tensor", "dp"),
        P("tensor", "dp"),
        P("dp", None),
        P(None, "tensor"),
        P("dp", None, None),
        P(),
        P(None, "tensor"),
        P("tensor", None),
    )
    out_specs = P("dp", None)
    return jax.shard_map(shards, mesh=mesh, in_specs=in_specs, out_specs=out_specs, check_vma=False)
```

time: 630 us -> 370 us (0.59)
  waiting for transfers between devices: 533 us -> 159 us
  starting transfers between devices: 0.24 us -> 65.3 us
  blocking collectives: 34.2 us -> 98.7 us
  matrix products: 45.8 us -> 25.3 us
    reduce_scatter x3 -> x0, waiting for transfers between devices: 285 us -> none  [the longest x1 129 us: shards(): lax.psum_scatter(partial_value.astype(jnp.bfloat16), 'tensor', scatter_di...]
    all_to_all x0 -> x4, blocking collectives: none -> 98.7 us  [the longest x1 35.2 us: shards(): q_wide = lax.all_to_all(q_wide, 'dp', 0, 0, tiled=True)]
    psum x1 -> x0, waiting for transfers between devices: 83 us -> none  [shards(): lax.psum(jnp.dot(inner, w_back, preferred_element_type=jnp.float32).astyp...]
    ppermute x0 -> x28, starting transfers between devices: none -> 60.7 us  [tensor_blocks(): return [x] + [lax.ppermute(x, 'tensor', pairs[j]) for j in range(1, 8)]]
    all_gather x1 -> x0, blocking collectives: 34.2 us -> none  [shards(): whole = lax.all_gather(attended, 'tensor', axis=1, tiled=True)]
    all_gather x3 -> x2, waiting for transfers between devices: 162 us -> 135 us  [the longest x1 101 us: shards(): down_all = lax.all_gather(w_down, 'dp', axis=1, tiled=True)]
    ppermute x0 -> x28, waiting for transfers between devices: none -> 23.4 us  [tensor_blocks(): return [x] + [lax.ppermute(x, 'tensor', pairs[j]) for j in range(1, 8)]]
    dot_general x8 -> x10, matrix products: 45.8 us -> 25.3 us  [the longest x7 21.3 us: matmul(): return jnp.dot(a, b, preferred_element_type=F32)]
  transfers between devices with their start and end apart: 7 -> 31, of which waited for: 7 -> 12; matrix products, arithmetic and copies ran while one was open for 5% -> 4% of each run, Pallas kernels for 0% -> 0%
where the time goes in v1:
time: 370 us
  waiting for transfers between devices  159 us (43%)
  blocking collectives  98.7 us (27%)
  starting transfers between devices  65.3 us (18%)
  matrix products  25.3 us (7%)
  between operations  13.9 us (4%)
  other arithmetic  4.81 us (1%)
    all_gather x1, waiting for transfers between devices, shards(): down_all = lax.all_gather(w_down, 'dp', axis=1, tiled=True)  101 us
    ppermute x28, starting transfers between devices, tensor_blocks(): return [x] + [lax.ppermute(x, 'tensor', pairs[j]) for j in range(1, 8)]  60.7 us
    all_to_all x1, blocking collectives, shards(): q_wide = lax.all_to_all(q_wide, 'dp', 0, 0, tiled=True)  35.2 us
    all_gather x1, waiting for transfers between devices, shards(): kv_all = lax.all_gather(w_kv, 'tensor', axis=0, tiled=True)  34.3 us
    all_to_all x1, blocking collectives, shards(): wide = lax.all_to_all(wide.astype(BF16), 'dp', 0, 0, tiled=True)  33.7 us
    ppermute x28, waiting for transfers between devices, tensor_blocks(): return [x] + [lax.ppermute(x, 'tensor', pairs[j]) for j in range(1, 8)]  23.4 us
    dot_general x7, matrix products, matmul(): return jnp.dot(a, b, preferred_element_type=F32)  21.3 us
    all_to_all x1, blocking collectives, shards(): part = lax.all_to_all(part.astype(BF16), 'tensor', 0, 0, tiled=True)  20.5 us
  transfers between devices with their start and end apart: 31, of which 12 were waited for; matrix products, arithmetic and copies ran while one was open for 4% of the time, Pallas kernels for 0%

profile of v1, /device:TPU:0, one launch (start us, length us, event | category | flops | bytes accessed | tf_op | source)
XLA Modules:
  0.0 369.9 jit_solution(4077458324201537001)
XLA Ops:
  6.5 1.2 copy.17
  7.8 1.1 copy.18
  10.8 1.6 constant_dynamic-update-slice_fusion.7
  12.3 2.1 collective-permute-start
  14.4 3.6 collective-permute-start.1
  18.0 3.0 collective-permute-start.3
  21.0 7.1 %collective-permute-start.5 = (bf16[32,256]{1,0:T(8,128)(2,1)S(1)}, bf16[32,256]{1,0:T(8,128)(2,1)S(1)}, u32[]{:S(2)}, u32[]{:S(2)}) collective-permute-start(bf16[32,256]{1,0:T(8,128)(2,1)S(1)} %get-tuple-element.8), channel_id=1, source_target_pairs={{0,6},{1,7},{2,4},{3,5},{4,2},{5,3},{6,0},{7,1},{8,14},{9,15},{10,... | collective-permute-start | bytes 49160 | tf_op jit(solution)/shard_map/ppermute | solution.py:29
  28.2 2.3 collective-permute-done.5
  30.5 5.1 %collective-permute-done.6 = bf16[32,256]{1,0:T(8,128)(2,1)S(1)} collective-permute-done((bf16[32,256]{1,0:T(8,128)(2,1)S(1)}, bf16[32,256]{1,0:T(8,128)(2,1)S(1)}, u32[]{:S(2)}, u32[]{:S(2)}) %collective-permute-start.6) | collective-permute-done | bytes 16416 | tf_op jit(solution)/shard_map/ppermute | solution.py:29
  36.4 4.6 %all-to-all-start = ((bf16[16,32,128]{2,1,0:T(8,128)(2,1)}), bf16[16,32,128]{2,1,0:T(8,128)(2,1)S(1)}, u32[]{:S(2)}, u32[]{:S(2)}) async-start(bf16[16,32,128]{2,1,0:T(8,128)(2,1)} %bitcast.8), calls=%async_computation | async-start | bytes 262144 | tf_op jit(solution)/shard_map/all_to_all | solution.py:56
  41.0 34.3 %all-gather.3.cloned.1.call-done = bf16[6144,256]{0,1:T(8,128)(2,1)} async-done(((bf16[768,256]{0,1:T(8,128)(2,1)}), bf16[6144,256]{0,1:T(8,128)(2,1)}) %all-gather.3.cloned.1.call-update) | async-done | bytes 3145744 | tf_op jit(solution)/shard_map/all_gather | solution.py:59
  75.3 100.8 %all-gather.5.cloned.1.call-done = bf16[1536,6144]{1,0:T(8,128)(2,1)} async-done(((bf16[1536,384]{1,0:T(8,128)(2,1)}), bf16[1536,6144]{1,0:T(8,128)(2,1)}) %all-gather.5.cloned.1.call-update) | async-done | bytes 18874384 | tf_op jit(solution)/shard_map/all_gather | solution.py:58
  176.1 10.0 %fusion = bf16[1536,256]{0,1:T(8,128)(2,1)S(1)} fusion(bf16[6144,256]{0,1:T(8,128)(2,1)} %all-gather.3.cloned.1.call-done, bf16[1536,6144]{1,0:T(8,128)(2,1)} %all-gather.5.cloned.1.call-done), kind=kOutput, calls=%fused_computation.3 | convolution fusion | flops 4832231424 | bytes 22806528 | tf_op jit(solution)/shard_map/dot_general | solution.py:20
  186.1 1.1 maximum_maximum_fusion
  187.2 1.8 convolution_convert_fusion
  189.0 35.2 %all_to_all.51 = bf16[16,32,2304]{2,1,0:T(8,128)(2,1)S(1)} all-to-all(bf16[16,32,2304]{2,1,0:T(8,128)(2,1)S(1)} %bitcast.102), channel_id=1, replica_groups=mesh['dp'=16,'tensor'=8] {'dp'}, dimensions={0} | all-to-all | bytes 4718592 | tf_op jit(solution)/shard_map/all_to_all | solution.py:62
  224.3 1.4 fusion.2
  225.7 0.8 add_convert_fusion
  226.5 20.5 %all_to_all.52 = bf16[8,64,768]{2,1,0:T(8,128)(2,1)S(1)} all-to-all(bf16[8,64,768]{2,1,0:T(8,128)(2,1)S(1)} %bitcast.112), channel_id=1, replica_groups=mesh['dp'=16,'tensor'=8] {'tensor'}, dimensions={0} | all-to-all | bytes 1572864 | tf_op jit(solution)/shard_map/all_to_all | solution.py:64
  247.9 2.1 collective-permute-start.8
  250.0 2.4 collective-permute-start.9
  253.0 1.3 collective-permute-start.11
  254.5 4.1 %collective-permute-start.12 = (bf16[64,768]{1,0:T(8,128)(2,1)S(1)}, bf16[64,768]{1,0:T(8,128)(2,1)S(1)}, u32[]{:S(2)}, u32[]{:S(2)}) collective-permute-start(bf16[64,768]{1,0:T(8,128)(2,1)S(1)} %divide_convert_fusion), channel_id=1, source_target_pairs={{0,6},{1,7},{2,4},{3,5},{4,2},{5,3},{6,0},{7,1},{8,14},{9,15},{10,... | collective-permute-start | bytes 294920 | tf_op jit(solution)/shard_map/ppermute | solution.py:29
  258.6 4.4 %collective-permute-start.13 = (bf16[64,768]{1,0:T(8,128)(2,1)S(1)}, bf16[64,768]{1,0:T(8,128)(2,1)S(1)}, u32[]{:S(2)}, u32[]{:S(2)}) collective-permute-start(bf16[64,768]{1,0:T(8,128)(2,1)S(1)} %divide_convert_fusion), channel_id=1, source_target_pairs={{0,7},{1,6},{2,5},{3,4},{4,3},{5,2},{6,1},{7,0},{8,15},{9,14},{10,... | collective-permute-start | bytes 294920 | tf_op jit(solution)/shard_map/ppermute | solution.py:29
  263.0 1.0 collective-permute-done.12
  264.0 3.0 collective-permute-done.13
  267.3 1.4 convolution_convert_fusion.1
  268.7 0.8 convolution_convert_fusion.4
  269.7 33.7 %all_to_all.53 = bf16[16,32,2304]{2,1,0:T(8,128)(2,1)S(1)} all-to-all(bf16[16,32,2304]{2,1,0:T(8,128)(2,1)S(1)} %pad_maximum_fusion), channel_id=1, replica_groups=mesh['dp'=16,'tensor'=8] {'dp'}, dimensions={0} | all-to-all | bytes 4718592 | tf_op jit(solution)/shard_map/all_to_all | solution.py:69
  304.2 9.3 %all_to_all.54 = bf16[16,32,128]{2,1,0:T(8,128)(2,1)S(1)} all-to-all(bf16[16,32,128]{2,1,0:T(8,128)(2,1)S(1)} %bitcast.115), channel_id=1, replica_groups=mesh['dp'=16,'tensor'=8] {'dp'}, dimensions={0} | all-to-all | bytes 262144 | tf_op jit(solution)/shard_map/all_to_all | solution.py:71
  313.6 3.2 collective-permute-start.15
  316.8 1.5 collective-permute-start.16
  318.3 2.5 collective-permute-start.17
  320.8 6.3 %collective-permute-start.19 = (bf16[32,2048]{1,0:T(8,128)(2,1)S(1)}, bf16[32,2048]{1,0:T(8,128)(2,1)S(1)}, u32[]{:S(2)}, u32[]{:S(2)}) collective-permute-start(bf16[32,2048]{1,0:T(8,128)(2,1)S(1)} %copy_bitcast_fusion), channel_id=1, source_target_pairs={{0,6},{1,7},{2,4},{3,5},{4,2},{5,3},{6,0},{7,1},{8,14},{9,15},{10,... | collective-permute-start | bytes 393224 | tf_op jit(solution)/shard_map/ppermute | solution.py:29
  327.1 1.3 collective-permute-start.20
  328.3 1.3 collective-permute-done.18
  329.6 4.6 %collective-permute-done.19 = bf16[32,2048]{1,0:T(8,128)(2,1)S(1)} collective-permute-done((bf16[32,2048]{1,0:T(8,128)(2,1)S(1)}, bf16[32,2048]{1,0:T(8,128)(2,1)S(1)}, u32[]{:S(2)}, u32[]{:S(2)}) %collective-permute-start.19) | collective-permute-done | bytes 131104 | tf_op jit(solution)/shard_map/ppermute | solution.py:29
  334.2 1.4 collective-permute-done.20
  335.7 1.7 fusion.40
  337.6 5.1 %convolution_convert_fusion.3 = bf16[32,2048]{1,0:T(8,128)(2,1)S(1)} fusion(bf16[1024,2048]{1,0:T(8,128)(2,1)} %param.21, bf16[2048,1024]{1,0:T(8,128)(2,1)} %param.20, f32[32,2048]{1,0:T(8,128)S(1)} %get-tuple-element.10, f32[32]{0:T(128)S(1)} %add_rsqrt_fusion, f32[32]{0:T(128)S(1)} %broadcast_multiply_fusion), kind=kOutput, calls=%fused_computation.7 | convolution fusion | flops 268992512 | bytes 8782080 | tf_op jit(solution)/shard_map/dot_general | solution.py:20
  342.8 2.3 collective-permute-start.22
  345.1 2.4 collective-permute-start.23
  347.5 1.3 collective-permute-start.24
  349.3 4.3 %collective-permute-start.26 = (bf16[32,2048]{1,0:T(8,128)(2,1)S(1)}, bf16[32,2048]{1,0:T(8,128)(2,1)S(1)}, u32[]{:S(2)}, u32[]{:S(2)}) collective-permute-start(bf16[32,2048]{1,0:T(8,128)(2,1)S(1)} %convolution_convert_fusion.3), channel_id=1, source_target_pairs={{0,6},{1,7},{2,4},{3,5},{4,2},{5,3},{6,0},{7,1},{8,14},{9,15},{10,... | collective-permute-start | bytes 393224 | tf_op jit(solution)/shard_map/ppermute | solution.py:29
  353.6 3.9 %collective-permute-start.27 = (bf16[32,2048]{1,0:T(8,128)(2,1)S(1)}, bf16[32,2048]{1,0:T(8,128)(2,1)S(1)}, u32[]{:S(2)}, u32[]{:S(2)}) collective-permute-start(bf16[32,2048]{1,0:T(8,128)(2,1)S(1)} %convolution_convert_fusion.3), channel_id=1, source_target_pairs={{0,7},{1,6},{2,5},{3,4},{4,3},{5,2},{6,1},{7,0},{8,15},{9,14},{10,... | collective-permute-start | bytes 393224 | tf_op jit(solution)/shard_map/ppermute | solution.py:29
  357.6 2.2 collective-permute-done.26
  359.8 2.4 collective-permute-done.27
  362.2 0.8 add_convert_fusion.1
  (97 shorter events, 6.5 us)
Async XLA Ops:
  6.5 217.8 %copy-start = (bf16[768,1536]{1,0:T(8,128)(2,1)S(1)}, bf16[768,1536]{1,0:T(8,128)(2,1)}, u32[]{:S(2)}) copy-start(bf16[768,1536]{1,0:T(8,128)(2,1)} %param.11) | copy-start | bytes 7077892
  6.5 3.9 %copy-start.1 = (f32[32,2048]{1,0:T(8,128)S(1)}, f32[32,2048]{1,0:T(8,128)}, u32[]{:S(2)}) copy-start(f32[32,2048]{1,0:T(8,128)} %param.16) | copy-start | bytes 786436
  6.5 68.8 %all-gather.3.cloned.1.call-start = ((), (), s32[]{:S(2)}) async-start(), calls=%async_computation.5 | async-start | bytes 3538944 | tf_op jit(solution)/shard_map/all_gather | solution.py:59
  9.6 166.5 %all-gather.5.cloned.1.call-start = ((), (), s32[]{:S(2)}) async-start(), calls=%async_computation.6 | async-start | bytes 20054016 | tf_op jit(solution)/shard_map/all_gather | solution.py:58
  12.3 8.7 %collective-permute-start = (bf16[32,256]{1,0:T(8,128)(2,1)S(1)}, bf16[32,256]{1,0:T(8,128)(2,1)S(1)}, u32[]{:S(2)}, u32[]{:S(2)}) collective-permute-start(bf16[32,256]{1,0:T(8,128)(2,1)S(1)} %get-tuple-element.8), channel_id=1, source_target_pairs={{0,1},{1,0},{2,3},{3,2},{4,5},{5,4},{6,7},{7,6},{8,9},{9,8},{10,11... | collective-permute-start | bytes 49160 | tf_op jit(solution)/shard_map/ppermute | solution.py:29
  14.4 13.7 %collective-permute-start.1 = (bf16[32,256]{1,0:T(8,128)(2,1)S(1)}, bf16[32,256]{1,0:T(8,128)(2,1)S(1)}, u32[]{:S(2)}, u32[]{:S(2)}) collective-permute-start(bf16[32,256]{1,0:T(8,128)(2,1)S(1)} %get-tuple-element.8), channel_id=1, source_target_pairs={{0,2},{1,3},{2,0},{3,1},{4,6},{5,7},{6,4},{7,5},{8,10},{9,11},{10,... | collective-permute-start | bytes 49160 | tf_op jit(solution)/shard_map/ppermute | solution.py:29
  18.0 10.2 %collective-permute-start.2 = (bf16[32,256]{1,0:T(8,128)(2,1)S(1)}, bf16[32,256]{1,0:T(8,128)(2,1)S(1)}, u32[]{:S(2)}, u32[]{:S(2)}) collective-permute-start(bf16[32,256]{1,0:T(8,128)(2,1)S(1)} %get-tuple-element.8), channel_id=1, source_target_pairs={{0,3},{1,2},{2,1},{3,0},{4,7},{5,6},{6,5},{7,4},{8,11},{9,10},{10,... | collective-permute-start | bytes 49160 | tf_op jit(solution)/shard_map/ppermute | solution.py:29
  18.0 10.2 %collective-permute-start.3 = (bf16[32,256]{1,0:T(8,128)(2,1)S(1)}, bf16[32,256]{1,0:T(8,128)(2,1)S(1)}, u32[]{:S(2)}, u32[]{:S(2)}) collective-permute-start(bf16[32,256]{1,0:T(8,128)(2,1)S(1)} %get-tuple-element.8), channel_id=1, source_target_pairs={{0,4},{1,5},{2,6},{3,7},{4,0},{5,1},{6,2},{7,3},{8,12},{9,13},{10,... | collective-permute-start | bytes 49160 | tf_op jit(solution)/shard_map/ppermute | solution.py:29
  21.0 7.2 %collective-permute-start.4 = (bf16[32,256]{1,0:T(8,128)(2,1)S(1)}, bf16[32,256]{1,0:T(8,128)(2,1)S(1)}, u32[]{:S(2)}, u32[]{:S(2)}) collective-permute-start(bf16[32,256]{1,0:T(8,128)(2,1)S(1)} %get-tuple-element.8), channel_id=1, source_target_pairs={{0,5},{1,4},{2,7},{3,6},{4,1},{5,0},{6,3},{7,2},{8,13},{9,12},{10,... | collective-permute-start | bytes 49160 | tf_op jit(solution)/shard_map/ppermute | solution.py:29
  21.0 9.4 %collective-permute-start.5 = (bf16[32,256]{1,0:T(8,128)(2,1)S(1)}, bf16[32,256]{1,0:T(8,128)(2,1)S(1)}, u32[]{:S(2)}, u32[]{:S(2)}) collective-permute-start(bf16[32,256]{1,0:T(8,128)(2,1)S(1)} %get-tuple-element.8), channel_id=1, source_target_pairs={{0,6},{1,7},{2,4},{3,5},{4,2},{5,3},{6,0},{7,1},{8,14},{9,15},{10,... | collective-permute-start | bytes 49160 | tf_op jit(solution)/shard_map/ppermute | solution.py:29
  28.1 7.5 %collective-permute-start.6 = (bf16[32,256]{1,0:T(8,128)(2,1)S(1)}, bf16[32,256]{1,0:T(8,128)(2,1)S(1)}, u32[]{:S(2)}, u32[]{:S(2)}) collective-permute-start(bf16[32,256]{1,0:T(8,128)(2,1)S(1)} %get-tuple-element.8), channel_id=1, source_target_pairs={{0,7},{1,6},{2,5},{3,4},{4,3},{5,2},{6,1},{7,0},{8,15},{9,14},{10,... | collective-permute-start | bytes 49160 | tf_op jit(solution)/shard_map/ppermute | solution.py:29
  36.4 150.8 %all-to-all-start = ((bf16[16,32,128]{2,1,0:T(8,128)(2,1)}), bf16[16,32,128]{2,1,0:T(8,128)(2,1)S(1)}, u32[]{:S(2)}, u32[]{:S(2)}) async-start(bf16[16,32,128]{2,1,0:T(8,128)(2,1)} %bitcast.8), calls=%async_computation | async-start | bytes 262144 | tf_op jit(solution)/shard_map/all_to_all | solution.py:56
  224.3 1.4 copy-start.4
  226.5 20.6 %copy-start.3 = (f32[1,32,768]{2,1,0:T(8,128)S(1)}, f32[1,32,768]{2,1,0:T(8,128)}, u32[]{:S(2)}) copy-start(f32[1,32,768]{2,1,0:T(8,128)} %param.18) | copy-start | bytes 294916
  247.6 6.9 %collective-permute-start.7 = (bf16[64,768]{1,0:T(8,128)(2,1)S(1)}, bf16[64,768]{1,0:T(8,128)(2,1)S(1)}, u32[]{:S(2)}, u32[]{:S(2)}) collective-permute-start(bf16[64,768]{1,0:T(8,128)(2,1)S(1)} %divide_convert_fusion), channel_id=1, source_target_pairs={{0,1},{1,0},{2,3},{3,2},{4,5},{5,4},{6,7},{7,6},{8,9},{9,8},{10,11... | collective-permute-start | bytes 294920 | tf_op jit(solution)/shard_map/ppermute | solution.py:29
  247.9 10.7 %collective-permute-start.8 = (bf16[64,768]{1,0:T(8,128)(2,1)S(1)}, bf16[64,768]{1,0:T(8,128)(2,1)S(1)}, u32[]{:S(2)}, u32[]{:S(2)}) collective-permute-start(bf16[64,768]{1,0:T(8,128)(2,1)S(1)} %divide_convert_fusion), channel_id=1, source_target_pairs={{0,2},{1,3},{2,0},{3,1},{4,6},{5,7},{6,4},{7,5},{8,10},{9,11},{10,... | collective-permute-start | bytes 294920 | tf_op jit(solution)/shard_map/ppermute | solution.py:29
  250.0 13.0 %collective-permute-start.9 = (bf16[64,768]{1,0:T(8,128)(2,1)S(1)}, bf16[64,768]{1,0:T(8,128)(2,1)S(1)}, u32[]{:S(2)}, u32[]{:S(2)}) collective-permute-start(bf16[64,768]{1,0:T(8,128)(2,1)S(1)} %divide_convert_fusion), channel_id=1, source_target_pairs={{0,3},{1,2},{2,1},{3,0},{4,7},{5,6},{6,5},{7,4},{8,11},{9,10},{10,... | collective-permute-start | bytes 294920 | tf_op jit(solution)/shard_map/ppermute | solution.py:29
  252.4 10.6 %collective-permute-start.10 = (bf16[64,768]{1,0:T(8,128)(2,1)S(1)}, bf16[64,768]{1,0:T(8,128)(2,1)S(1)}, u32[]{:S(2)}, u32[]{:S(2)}) collective-permute-start(bf16[64,768]{1,0:T(8,128)(2,1)S(1)} %divide_convert_fusion), channel_id=1, source_target_pairs={{0,4},{1,5},{2,6},{3,7},{4,0},{5,1},{6,2},{7,3},{8,12},{9,13},{10,... | collective-permute-start | bytes 294920 | tf_op jit(solution)/shard_map/ppermute | solution.py:29
  253.0 10.0 %collective-permute-start.11 = (bf16[64,768]{1,0:T(8,128)(2,1)S(1)}, bf16[64,768]{1,0:T(8,128)(2,1)S(1)}, u32[]{:S(2)}, u32[]{:S(2)}) collective-permute-start(bf16[64,768]{1,0:T(8,128)(2,1)S(1)} %divide_convert_fusion), channel_id=1, source_target_pairs={{0,5},{1,4},{2,7},{3,6},{4,1},{5,0},{6,3},{7,2},{8,13},{9,12},{10,... | collective-permute-start | bytes 294920 | tf_op jit(solution)/shard_map/ppermute | solution.py:29
  254.5 9.5 %collective-permute-start.12 = (bf16[64,768]{1,0:T(8,128)(2,1)S(1)}, bf16[64,768]{1,0:T(8,128)(2,1)S(1)}, u32[]{:S(2)}, u32[]{:S(2)}) collective-permute-start(bf16[64,768]{1,0:T(8,128)(2,1)S(1)} %divide_convert_fusion), channel_id=1, source_target_pairs={{0,6},{1,7},{2,4},{3,5},{4,2},{5,3},{6,0},{7,1},{8,14},{9,15},{10,... | collective-permute-start | bytes 294920 | tf_op jit(solution)/shard_map/ppermute | solution.py:29
  258.6 8.5 %collective-permute-start.13 = (bf16[64,768]{1,0:T(8,128)(2,1)S(1)}, bf16[64,768]{1,0:T(8,128)(2,1)S(1)}, u32[]{:S(2)}, u32[]{:S(2)}) collective-permute-start(bf16[64,768]{1,0:T(8,128)(2,1)S(1)} %divide_convert_fusion), channel_id=1, source_target_pairs={{0,7},{1,6},{2,5},{3,4},{4,3},{5,2},{6,1},{7,0},{8,15},{9,14},{10,... | collective-permute-start | bytes 294920 | tf_op jit(solution)/shard_map/ppermute | solution.py:29
  268.7 67.0 %slice-start = ((s8[8388608]{0:T(1024)(128)(4,1)}), s8[4194304]{0:T(1024)(128)(4,1)S(1)}, s32[]{:S(2)}) async-start(s8[8388608]{0:T(1024)(128)(4,1)} %bitcast.103), calls=%async_computation.7 | async-start | bytes 8388608
  269.5 33.9 %copy-start.2 = (bf16[2304,256]{0,1:T(8,128)(2,1)S(1)}, bf16[2304,256]{0,1:T(8,128)(2,1)}, u32[]{:S(2)}) copy-start(bf16[2304,256]{0,1:T(8,128)(2,1)} %maximum_maximum_fusion) | copy-start | bytes 3538948
  269.7 66.0 %slice-start.1 = ((s8[8388608]{0:T(1024)(128)(4,1)}), s8[4194304]{0:T(1024)(128)(4,1)S(1)}, s32[]{:S(2)}) async-start(s8[8388608]{0:T(1024)(128)(4,1)} %bitcast.103), calls=%async_computation.8 | async-start | bytes 8388608
  313.5 7.3 %collective-permute-start.14 = (bf16[32,2048]{1,0:T(8,128)(2,1)S(1)}, bf16[32,2048]{1,0:T(8,128)(2,1)S(1)}, u32[]{:S(2)}, u32[]{:S(2)}) collective-permute-start(bf16[32,2048]{1,0:T(8,128)(2,1)S(1)} %copy_bitcast_fusion), channel_id=1, source_target_pairs={{0,1},{1,0},{2,3},{3,2},{4,5},{5,4},{6,7},{7,6},{8,9},{9,8},{10,11... | collective-permute-start | bytes 393224 | tf_op jit(solution)/shard_map/ppermute | solution.py:29
  313.6 13.5 %collective-permute-start.15 = (bf16[32,2048]{1,0:T(8,128)(2,1)S(1)}, bf16[32,2048]{1,0:T(8,128)(2,1)S(1)}, u32[]{:S(2)}, u32[]{:S(2)}) collective-permute-start(bf16[32,2048]{1,0:T(8,128)(2,1)S(1)} %copy_bitcast_fusion), channel_id=1, source_target_pairs={{0,2},{1,3},{2,0},{3,1},{4,6},{5,7},{6,4},{7,5},{8,10},{9,11},{10,... | collective-permute-start | bytes 393224 | tf_op jit(solution)/shard_map/ppermute | solution.py:29
  316.8 11.5 %collective-permute-start.16 = (bf16[32,2048]{1,0:T(8,128)(2,1)S(1)}, bf16[32,2048]{1,0:T(8,128)(2,1)S(1)}, u32[]{:S(2)}, u32[]{:S(2)}) collective-permute-start(bf16[32,2048]{1,0:T(8,128)(2,1)S(1)} %copy_bitcast_fusion), channel_id=1, source_target_pairs={{0,3},{1,2},{2,1},{3,0},{4,7},{5,6},{6,5},{7,4},{8,11},{9,10},{10,... | collective-permute-start | bytes 393224 | tf_op jit(solution)/shard_map/ppermute | solution.py:29
  318.3 10.1 %collective-permute-start.17 = (bf16[32,2048]{1,0:T(8,128)(2,1)S(1)}, bf16[32,2048]{1,0:T(8,128)(2,1)S(1)}, u32[]{:S(2)}, u32[]{:S(2)}) collective-permute-start(bf16[32,2048]{1,0:T(8,128)(2,1)S(1)} %copy_bitcast_fusion), channel_id=1, source_target_pairs={{0,4},{1,5},{2,6},{3,7},{4,0},{5,1},{6,2},{7,3},{8,12},{9,13},{10,... | collective-permute-start | bytes 393224 | tf_op jit(solution)/shard_map/ppermute | solution.py:29
  320.8 8.8 %collective-permute-start.18 = (bf16[32,2048]{1,0:T(8,128)(2,1)S(1)}, bf16[32,2048]{1,0:T(8,128)(2,1)S(1)}, u32[]{:S(2)}, u32[]{:S(2)}) collective-permute-start(bf16[32,2048]{1,0:T(8,128)(2,1)S(1)} %copy_bitcast_fusion), channel_id=1, source_target_pairs={{0,5},{1,4},{2,7},{3,6},{4,1},{5,0},{6,3},{7,2},{8,13},{9,12},{10,... | collective-permute-start | bytes 393224 | tf_op jit(solution)/shard_map/ppermute | solution.py:29
  320.8 13.5 %collective-permute-start.19 = (bf16[32,2048]{1,0:T(8,128)(2,1)S(1)}, bf16[32,2048]{1,0:T(8,128)(2,1)S(1)}, u32[]{:S(2)}, u32[]{:S(2)}) collective-permute-start(bf16[32,2048]{1,0:T(8,128)(2,1)S(1)} %copy_bitcast_fusion), channel_id=1, source_target_pairs={{0,6},{1,7},{2,4},{3,5},{4,2},{5,3},{6,0},{7,1},{8,14},{9,15},{10,... | collective-permute-start | bytes 393224 | tf_op jit(solution)/shard_map/ppermute | solution.py:29
  327.1 8.6 %collective-permute-start.20 = (bf16[32,2048]{1,0:T(8,128)(2,1)S(1)}, bf16[32,2048]{1,0:T(8,128)(2,1)S(1)}, u32[]{:S(2)}, u32[]{:S(2)}) collective-permute-start(bf16[32,2048]{1,0:T(8,128)(2,1)S(1)} %copy_bitcast_fusion), channel_id=1, source_target_pairs={{0,7},{1,6},{2,5},{3,4},{4,3},{5,2},{6,1},{7,0},{8,15},{9,14},{10,... | collective-permute-start | bytes 393224 | tf_op jit(solution)/shard_map/ppermute | solution.py:29
  342.7 6.6 %collective-permute-start.21 = (bf16[32,2048]{1,0:T(8,128)(2,1)S(1)}, bf16[32,2048]{1,0:T(8,128)(2,1)S(1)}, u32[]{:S(2)}, u32[]{:S(2)}) collective-permute-start(bf16[32,2048]{1,0:T(8,128)(2,1)S(1)} %convolution_convert_fusion.3), channel_id=1, source_target_pairs={{0,1},{1,0},{2,3},{3,2},{4,5},{5,4},{6,7},{7,6},{8,9},{9,8},{10,11... | collective-permute-start | bytes 393224 | tf_op jit(solution)/shard_map/ppermute | solution.py:29
  342.8 10.9 %collective-permute-start.22 = (bf16[32,2048]{1,0:T(8,128)(2,1)S(1)}, bf16[32,2048]{1,0:T(8,128)(2,1)S(1)}, u32[]{:S(2)}, u32[]{:S(2)}) collective-permute-start(bf16[32,2048]{1,0:T(8,128)(2,1)S(1)} %convolution_convert_fusion.3), channel_id=1, source_target_pairs={{0,2},{1,3},{2,0},{3,1},{4,6},{5,7},{6,4},{7,5},{8,10},{9,11},{10,... | collective-permute-start | bytes 393224 | tf_op jit(solution)/shard_map/ppermute | solution.py:29
  345.1 12.5 %collective-permute-start.23 = (bf16[32,2048]{1,0:T(8,128)(2,1)S(1)}, bf16[32,2048]{1,0:T(8,128)(2,1)S(1)}, u32[]{:S(2)}, u32[]{:S(2)}) collective-permute-start(bf16[32,2048]{1,0:T(8,128)(2,1)S(1)} %convolution_convert_fusion.3), channel_id=1, source_target_pairs={{0,3},{1,2},{2,1},{3,0},{4,7},{5,6},{6,5},{7,4},{8,11},{9,10},{10,... | collective-permute-start | bytes 393224 | tf_op jit(solution)/shard_map/ppermute | solution.py:29
  347.5 10.1 %collective-permute-start.24 = (bf16[32,2048]{1,0:T(8,128)(2,1)S(1)}, bf16[32,2048]{1,0:T(8,128)(2,1)S(1)}, u32[]{:S(2)}, u32[]{:S(2)}) collective-permute-start(bf16[32,2048]{1,0:T(8,128)(2,1)S(1)} %convolution_convert_fusion.3), channel_id=1, source_target_pairs={{0,4},{1,5},{2,6},{3,7},{4,0},{5,1},{6,2},{7,3},{8,12},{9,13},{10,... | collective-permute-start | bytes 393224 | tf_op jit(solution)/shard_map/ppermute | solution.py:29
  348.8 8.8 %collective-permute-start.25 = (bf16[32,2048]{1,0:T(8,128)(2,1)S(1)}, bf16[32,2048]{1,0:T(8,128)(2,1)S(1)}, u32[]{:S(2)}, u32[]{:S(2)}) collective-permute-start(bf16[32,2048]{1,0:T(8,128)(2,1)S(1)} %convolution_convert_fusion.3), channel_id=1, source_target_pairs={{0,5},{1,4},{2,7},{3,6},{4,1},{5,0},{6,3},{7,2},{8,13},{9,12},{10,... | collective-permute-start | bytes 393224 | tf_op jit(solution)/shard_map/ppermute | solution.py:29
  349.3 10.5 %collective-permute-start.26 = (bf16[32,2048]{1,0:T(8,128)(2,1)S(1)}, bf16[32,2048]{1,0:T(8,128)(2,1)S(1)}, u32[]{:S(2)}, u32[]{:S(2)}) collective-permute-start(bf16[32,2048]{1,0:T(8,128)(2,1)S(1)} %convolution_convert_fusion.3), channel_id=1, source_target_pairs={{0,6},{1,7},{2,4},{3,5},{4,2},{5,3},{6,0},{7,1},{8,14},{9,15},{10,... | collective-permute-start | bytes 393224 | tf_op jit(solution)/shard_map/ppermute | solution.py:29
  353.6 8.6 %collective-permute-start.27 = (bf16[32,2048]{1,0:T(8,128)(2,1)S(1)}, bf16[32,2048]{1,0:T(8,128)(2,1)S(1)}, u32[]{:S(2)}, u32[]{:S(2)}) collective-permute-start(bf16[32,2048]{1,0:T(8,128)(2,1)S(1)} %convolution_convert_fusion.3), channel_id=1, source_target_pairs={{0,7},{1,6},{2,5},{3,4},{4,3},{5,2},{6,1},{7,0},{8,15},{9,14},{10,... | collective-permute-start | bytes 393224 | tf_op jit(solution)/shard_map/ppermute | solution.py:29
Sparse Core Ops, SparseCore 0:
  9.8 65.5 all-gather.2
  77.0 99.0 all-gather.4
